TPU v7x, 256 devices: a whole 4x4x8 slice. The times are simulated.
256 devices in a mesh: dp: 8 (over y, core), vocab: 32 (over z, x).
Axes of the slice: x: 4, y: 4, z: 8, core: 2. Of those that a mesh axis runs over, the one named last changes fastest.
Arguments:
- token_grads: bfloat16 [524288, 1024], P(('dp', 'vocab')), may hold values from -6 to 6
- token_ids: int32 [524288], P(('dp', 'vocab')), may hold values from 0 to 125183, as said below
Outputs:
- delta_grad: float32 [125184, 1024], P('vocab', 'dp')
Inputs may be any that keep to these rules, and one draw needn't show every extreme that they name: `token_ids`: ids are skewed toward a few common ones within each shard of 3912 consecutive ids. Among the rows of one device at most 96 ids lie in one shard, and exactly 96 lie in one shard, the same shard for every device of a data group.
All inputs are finite; a program needn't handle non-finite values.
Results may differ from a plain program's by a relative error of at most 0.0003.
Values may be sent and summed in bfloat16 or wider, within the bound.
A program may use at most 128 MiB of HBM per device.

v0:
```python
import jax
import jax.numpy as jnp
from jax import lax
from jax.sharding import PartitionSpec as P

VSH = 3912


def body(token_grads, token_ids):
    shards = lax.axis_size("vocab")
    rows_dev = token_ids.shape[0]
    width = token_grads.shape[1]
    capacity = 3 * rows_dev // (2 * shards)
    owner = token_ids // VSH
    local = token_ids - owner * VSH
    marks = (owner[:, None] == jnp.arange(shards, dtype=jnp.int32)[None, :]).astype(jnp.int32)
    before = jnp.cumsum(marks, axis=0) - marks
    rank = jnp.sum(before * marks, axis=1)
    slot = owner * capacity + rank
    send_rows = jnp.zeros((shards * capacity, width), jnp.bfloat16).at[slot].set(token_grads)
    send_ids = jnp.zeros((shards * capacity,), jnp.int32).at[slot].set(local)
    got_rows, got_ids = (
        lax.all_to_all(
            send_rows.reshape(shards, capacity, width),
            "vocab",
            split_axis=0,
            concat_axis=0,
            tiled=True,
        ),
        lax.all_to_all(
            send_ids.reshape(shards, capacity), "vocab", split_axis=0, concat_axis=0, tiled=True
        ),
    )
    got_rows = got_rows.reshape(shards * capacity, width)
    got_ids = got_ids.reshape(shards * capacity)
    partial_sum = jax.ops.segment_sum(got_rows.astype(jnp.float32), got_ids, num_segments=VSH)
    return lax.psum_scatter(partial_sum, "dp", scatter_dimension=1, tiled=True)


def solution(mesh):
    return jax.shard_map(
        body,
        mesh=mesh,
        in_specs=(P(("dp", "vocab"), None), P(("dp", "vocab"))),
        out_specs=P("vocab", "dp"),
        check_vma=False,
    )
```

profile of v0, /device:TPU:1, one launch (start us, length us, event | category | flops | bytes accessed | tf_op | source)
XLA Modules:
  0.0 336.2 jit_solution(11465410394358558884)
XLA Ops:
  6.5 0.7 add_select_fusion
  7.3 9.1 %reduce-window.6 = s32[32,16,128]{2,1,0:T(8,128)S(1)} reduce-window(s32[32,16,128]{2,1,0:T(8,128)S(1)} %fusion.8, s32[]{:T(128)} %constant.9.clone.1), window={size=1x1x128 pad=0_0x0_0x127_0}, to_apply=%region_0.1 | reduce-window | flops 8323072 | bytes 524292 | tf_op jit(solution)/shard_map/reduce-window
  16.4 0.1 slice.8
  16.5 0.2 copy.5
  16.7 0.2 reduce-window.9
  16.9 0.1 broadcast_add_fusion
  17.1 0.1 fusion.7
  17.2 0.7 multiply_subtract_fusion
  17.9 8.1 %scatter_custom_fusion = s32[3072]{0:T(1024)S(1)} fusion(s32[2048]{0:T(1024)S(1)} %get-tuple-element.6, s32[2048]{0:T(1024)S(1)} %get-tuple-element.5, s32[]{:T(128)} %constant.9.clone.1), kind=kCustom, calls=%fused_computation.22 | custom fusion | bytes 12292 | tf_op jit(solution)/shard_map/scatter | solution.py:21
  26.0 0.7 all_to_all.9
  26.7 11.9 %all-to-all-start = ((s32[32,1,96]{2,1,0:T(1,128)}), s32[32,1,96]{2,1,0:T(1,128)S(1)}, u32[]{:S(2)}, u32[]{:S(2)}) async-start(s32[32,1,96]{2,1,0:T(1,128)} %all_to_all.9), calls=%async_computation | async-start | bytes 32768 | tf_op jit(solution)/shard_map/all_to_all | solution.py:30
  38.5 14.2 %scatter_custom_fusion.1 = bf16[3072,1024]{1,0:T(8,128)(2,1)} fusion(s32[2048]{0:T(1024)S(1)} %get-tuple-element.6, bf16[2048,1024]{1,0:T(8,128)(2,1)} %param.2, bf16[]{:T(256)} %constant.26.clone.1), kind=kCustom, calls=%fused_computation.6 | custom fusion | bytes 6291968 | tf_op jit(solution)/shard_map/scatter | solution.py:20
  52.8 0.0 all-to-all-done
  52.8 9.3 %all-to-all-start.1 = ((bf16[32,96,1024]{2,1,0:T(8,128)(2,1)}), bf16[32,96,1024]{2,1,0:T(8,128)(2,1)}, u32[]{:S(2)}, u32[]{:S(2)}) async-start(bf16[32,96,1024]{2,1,0:T(8,128)(2,1)} %bitcast.27), calls=%async_computation.1 | async-start | bytes 12582912 | tf_op jit(solution)/shard_map/all_to_all | solution.py:23
  62.1 0.2 reduce-scatter.2.cloned.1.call-start
  62.3 0.5 broadcast.29
  62.9 0.7 reduce.3
  63.5 0.1 reshape.48
  63.6 134.5 %all-to-all-done.1 = bf16[32,96,1024]{2,1,0:T(8,128)(2,1)} async-done(((bf16[32,96,1024]{2,1,0:T(8,128)(2,1)}), bf16[32,96,1024]{2,1,0:T(8,128)(2,1)}, u32[]{:S(2)}, u32[]{:S(2)}) %all-to-all-start.1) | async-done | bytes 6291488 | tf_op jit(solution)/shard_map/all_to_all | solution.py:23
  198.1 33.1 %scatter_custom_fusion.2 = f32[3912,1024]{1,0:T(8,128)} fusion(s32[3072]{0:T(1024)S(1)} %reshape.48, bf16[3072,1024]{1,0:T(8,128)(2,1)} %bitcast.6, f32[]{:T(128)} %constant.8.clone.1), kind=kCustom, calls=%fused_computation.3 | custom fusion | flops 6291456 | bytes 22315012 | tf_op jit(solution)/shard_map/scatter-add | solution.py:36
  231.1 0.0 reduce-scatter.2.cloned.1.call-update
  231.2 98.2 %reduce-scatter.2.cloned.1.call-done = f32[3912,128]{1,0:T(8,128)} async-done(((f32[3912,1024]{1,0:T(8,128)}), f32[3912,128]{1,0:T(8,128)}) %reduce-scatter.2.cloned.1.call-update) | async-done | bytes 2002960 | tf_op jit(solution)/shard_map/reduce_scatter | solution.py:37
  (1 shorter events, 0.0 us)
Async XLA Ops:
  26.7 26.1 %all-to-all-start = ((s32[32,1,96]{2,1,0:T(1,128)}), s32[32,1,96]{2,1,0:T(1,128)S(1)}, u32[]{:S(2)}, u32[]{:S(2)}) async-start(s32[32,1,96]{2,1,0:T(1,128)} %all_to_all.9), calls=%async_computation | async-start | bytes 32768 | tf_op jit(solution)/shard_map/all_to_all | solution.py:30
  52.8 145.3 %all-to-all-start.1 = ((bf16[32,96,1024]{2,1,0:T(8,128)(2,1)}), bf16[32,96,1024]{2,1,0:T(8,128)(2,1)}, u32[]{:S(2)}, u32[]{:S(2)}) async-start(bf16[32,96,1024]{2,1,0:T(8,128)(2,1)} %bitcast.27), calls=%async_computation.1 | async-start | bytes 12582912 | tf_op jit(solution)/shard_map/all_to_all | solution.py:23
  62.1 267.3 %reduce-scatter.2.cloned.1.call-start = ((), (), s32[]{:S(2)}) async-start(), calls=%async_computation.3 | async-start | bytes 18026496 | tf_op jit(solution)/shard_map/reduce_scatter | solution.py:37
Sparse Core Ops, SparseCore 0:
  231.3 98.0 reduce-scatter.1
where the time goes:
time: 337 us; the launch traced here: 336 us
  waiting for transfers between devices  233 us (69%)
  other arithmetic  44.7 us (13%)
  local copies, waits for them, and re-layouts  23.9 us (7%)
  starting transfers between devices  21.4 us (6%)
  between operations  13.5 us (4%)
    all_to_all x1, waiting for transfers between devices, body(): lax.all_to_all(send_rows.reshape(shards, capacity, width), 'vocab', split...  134 us
    reduce_scatter x1, waiting for transfers between devices, body(): return lax.psum_scatter(partial_sum, 'dp', scatter_dimension=1, tiled=True)  98.2 us
    scatter-add x1, other arithmetic, body(): jax.ops.segment_sum(got_rows.astype(jnp.float32), got_ids, num_segments=VSH)  33.1 us
    scatter x1, local copies, waits for them, and re-layouts, body(): jnp.zeros((shards * capacity, width), jnp.bfloat16).at[slot]  14.2 us
    all_to_all x1, starting transfers between devices, body(): lax.all_to_all(send_ids.reshape(shards, capacity), 'vocab', split_axis=0,...  11.9 us
    another operation x3, other arithmetic  9.41 us
    all_to_all x1, starting transfers between devices, body(): lax.all_to_all(send_rows.reshape(shards, capacity, width), 'vocab', split...  9.33 us
    scatter x1, local copies, waits for them, and re-layouts, body(): send_ids = jnp.zeros((shards * capacity,), jnp.int32).at[slot].set(local)  8.06 us
  transfers between devices with their start and end apart: 3, of which 2 were waited for; matrix products, arithmetic and copies ran while one was open for 5% of the time, Pallas kernels for 0%

commit v1 on v0

v1 whole, which is shorter than its diff:
```python
import functools

import jax
import jax.numpy as jnp
from jax import lax
from jax.experimental import pallas as pl
from jax.experimental.pallas import tpu as pltpu
from jax.sharding import PartitionSpec as P

MESH = pl.DeviceIdType.MESH
VSH = 3912
SHARDS = 32
CAP = 96
ROWS = 2048
CHUNK = 784
CHUNKS = 5
QUARTER = 256
HALF = 128
BATCHES = 8
PEERS = 128


def place():
    dp, vocab = lax.axis_index("dp"), lax.axis_index("vocab")
    return dp // 2, dp % 2, vocab // 4, vocab % 4


def target(b, i, dy):
    y, c, z, x = place()
    to_z = (z + 2 * i + b % 2) % 8
    to_x = (x + i + b // 2) % 4
    to_y = (y + dy) % 4
    return (to_y * 2 + c, to_z * 4 + to_x), to_y, to_z * 4 + to_x


def rank_rows(ids_ref, rank, parts):
    ids = ids_ref[...]
    first = lax.broadcasted_iota(jnp.int32, (SHARDS, 1), 0) * VSH
    local = ids - first
    inside = (local >= 0) & (local < VSH)
    mine = jnp.sum(jnp.where(inside, local, 0), axis=0, keepdims=True)
    row = lax.broadcasted_iota(jnp.int32, (16, ROWS), 0)
    hi, lo = mine >> 6, mine & 63
    parts[...] = jnp.where(row == 0, hi, jnp.where(row == 1, lo, 0)).astype(jnp.float32).astype(jnp.bfloat16)
    block = 256
    before = lax.broadcasted_iota(jnp.int32, (block, block), 0) < lax.broadcasted_iota(jnp.int32, (block, block), 1)
    before = jnp.where(before, 1.0, 0.0).astype(jnp.bfloat16)
    carry = jnp.zeros((SHARDS, 1), jnp.float32)
    marks = jnp.where(inside, 1.0, 0.0)
    for k in range(ROWS // block):
        m = marks[:, k * block : (k + 1) * block]
        count = jnp.dot(m.astype(jnp.bfloat16), before, preferred_element_type=jnp.float32) + carry
        rank[:, k * block : (k + 1) * block] = jnp.where(m > 0.5, count, -1.0).astype(jnp.int32)
        carry = carry + jnp.sum(m, axis=1, keepdims=True)


def kernel(cap, ids_ref, grads_ref, out_ref, rank, parts, send, send_ids, recv, recv_ids, acc, other, ssem, isem, rsem, jsem, psem, qsem):
    y, c, z, x = place()
    partner = (y * 2 + 1 - c, z * 4 + x)
    barrier = pltpu.get_barrier_semaphore()

    def greet(j, _):
        peer, _, _ = target(j // 16, j // 4 % 4, j % 4)
        pl.semaphore_signal(barrier, inc=1, device_id=peer, device_id_type=MESH)
        return 0

    lax.fori_loop(1, PEERS, greet, 0)
    pl.semaphore_signal(barrier, inc=1, device_id=partner, device_id_type=MESH)
    rank_rows(ids_ref, rank, parts)
    send_ids[...] = jnp.zeros_like(send_ids)
    pl.semaphore_wait(barrier, PEERS)

    def rows_copy(b, i, dy):
        peer, _, _ = target(b, i, dy)
        j = b * 16 + i * 4 + dy
        return pltpu.make_async_remote_copy(send.at[j], recv.at[j], ssem.at[j], rsem.at[j], device_id=peer, device_id_type=MESH)

    def ids_copy(b, i, dy):
        peer, _, _ = target(b, i, dy)
        j = b * 16 + i * 4 + dy
        return pltpu.make_async_remote_copy(
            send_ids.at[b * 4 + i], recv_ids.at[j], isem.at[j], jsem.at[j], device_id=peer, device_id_type=MESH
        )

    own_rows = pltpu.make_async_copy(send.at[0], recv.at[0], rsem.at[0])
    own_ids = pltpu.make_async_copy(send_ids.at[0], recv_ids.at[0], jsem.at[0])

    def pack(b, _):
        picks = []
        slot = lax.broadcasted_iota(jnp.int32, (cap, ROWS), 0)
        for i in range(4):
            _, _, shard = target(b, i, 0)
            pick = jnp.where(rank[pl.ds(shard, 1), :] == slot, 1.0, 0.0).astype(jnp.bfloat16)
            pair = lax.dot_general(parts[...], pick, (((1,), (1,)), ((), ())), preferred_element_type=jnp.float32)
            local = (pair[0:1] * 64.0 + pair[1:2]).astype(jnp.int32)
            send_ids[b * 4 + i, :, 0:cap] = local
            picks.append(pick)
        picks = jnp.concatenate(picks, axis=0)
        for dy in range(4):
            _, to_y, _ = target(b, 0, dy)
            cols = pl.ds(pl.multiple_of(to_y * QUARTER, QUARTER), QUARTER)
            packed = jnp.dot(picks, grads_ref[:, cols], preferred_element_type=jnp.float32).astype(jnp.bfloat16)
            for i in range(4):
                send[b * 16 + i * 4 + dy] = packed[i * cap : (i + 1) * cap]
                if i == 0 and dy == 0:

                    @pl.when(b == 0)
                    def _():
                        own_rows.start()
                        own_ids.start()

                    @pl.when(b > 0)
                    def _():
                        rows_copy(b, 0, 0).start()
                        ids_copy(b, 0, 0).start()
                else:
                    rows_copy(b, i, dy).start()
                    ids_copy(b, i, dy).start()
        return 0

    lax.fori_loop(0, BATCHES, pack, 0)

    def chunk_sum(b, t, ids):
        start = pl.multiple_of(t * CHUNK, 16)
        row = lax.broadcasted_iota(jnp.int32, (CHUNK, 16 * cap), 0)
        hit = jnp.where(row == ids - start, 1.0, 0.0).astype(jnp.bfloat16)
        return start, jnp.dot(hit, recv[pl.ds(b * 16, 16)].reshape(16 * cap, QUARTER), preferred_element_type=jnp.float32)

    def arrive(b):
        def wait(k, _):
            rows_copy(b, k // 4, k % 4).wait_recv()
            ids_copy(b, k // 4, k % 4).wait_recv()
            return 0

        if isinstance(b, int) and b == 0:
            own_rows.wait()
            own_ids.wait()
            lax.fori_loop(1, 16, wait, 0)
        else:
            lax.fori_loop(0, 16, wait, 0)
        return jnp.concatenate([recv_ids[b * 16 + k][:, 0:cap] for k in range(16)], axis=1)

    def exchange(t):
        rows = pl.ds(pl.multiple_of(t * CHUNK, 16), CHUNK)
        return pltpu.make_async_remote_copy(
            acc.at[1 - c, rows], other.at[rows], psem.at[t], qsem.at[t], device_id=partner, device_id_type=MESH
        )

    def add(b, t, ids, fresh=False):
        start, part = chunk_sum(b, t, ids)
        rows = pl.ds(start, CHUNK)
        if fresh:
            acc[0, rows] = part[:, :HALF]
            acc[1, rows] = part[:, HALF:]
        else:
            acc[0, rows] += part[:, :HALF]
            acc[1, rows] += part[:, HALF:]

    def first(t, ids):
        add(0, t, ids, fresh=True)
        return ids

    def later(b, _):
        ids = arrive(b)

        def step(t, ids):
            add(b, t, ids)
            return ids

        lax.fori_loop(0, CHUNKS, step, ids)
        return 0

    def last(t, ids):
        add(BATCHES - 1, t, ids)
        exchange(t).start()
        return ids

    lax.fori_loop(0, CHUNKS, first, arrive(0))
    lax.fori_loop(1, BATCHES - 1, later, 0)
    lax.fori_loop(0, CHUNKS, last, arrive(BATCHES - 1))

    for t in range(CHUNKS):
        exchange(t).wait()
        n = min(CHUNK, VSH - t * CHUNK)
        out_ref[t * CHUNK : t * CHUNK + n] = acc[c, t * CHUNK : t * CHUNK + n] + other[t * CHUNK : t * CHUNK + n]

    def drain(j, _):
        rows_copy(j // 16, j // 4 % 4, j % 4).wait_send()
        ids_copy(j // 16, j // 4 % 4, j % 4).wait_send()
        return 0

    lax.fori_loop(1, PEERS, drain, 0)


def body(token_grads, token_ids):
    cap = CAP
    return pl.pallas_call(
        functools.partial(kernel, cap),
        out_shape=jax.ShapeDtypeStruct((VSH, HALF), jnp.float32),
        in_specs=[pl.BlockSpec(memory_space=pltpu.VMEM)] * 2,
        out_specs=pl.BlockSpec(memory_space=pltpu.VMEM),
        scratch_shapes=[
            pltpu.VMEM((SHARDS, ROWS), jnp.int32),
            pltpu.VMEM((16, ROWS), jnp.bfloat16),
            pltpu.VMEM((PEERS, cap, QUARTER), jnp.bfloat16),
            pltpu.VMEM((SHARDS, 1, 128), jnp.int32),
            pltpu.VMEM((PEERS, cap, QUARTER), jnp.bfloat16),
            pltpu.VMEM((PEERS, 1, 128), jnp.int32),
            pltpu.VMEM((2, CHUNK * CHUNKS, HALF), jnp.float32),
            pltpu.VMEM((CHUNK * CHUNKS, HALF), jnp.float32),
            pltpu.SemaphoreType.DMA((PEERS,)),
            pltpu.SemaphoreType.DMA((PEERS,)),
            pltpu.SemaphoreType.DMA((PEERS,)),
            pltpu.SemaphoreType.DMA((PEERS,)),
            pltpu.SemaphoreType.DMA((CHUNKS,)),
            pltpu.SemaphoreType.DMA((CHUNKS,)),
        ],
        compiler_params=pltpu.CompilerParams(collective_id=0, has_side_effects=True, vmem_limit_bytes=56 << 20),
        name="delta_grad",
    )(token_ids.reshape(1, ROWS), token_grads)


def solution(mesh):
    return jax.shard_map(
        body,
        mesh=mesh,
        in_specs=(P(("dp", "vocab"), None), P(("dp", "vocab"))),
        out_specs=P("vocab", "dp"),
        check_vma=False,
    )
```

time: 337 us -> 176 us (0.52)
  waiting for transfers between devices: 233 us -> 0 us
  Pallas kernels: 0 us -> 173 us
  other arithmetic: 44.7 us -> 0 us
  starting transfers between devices: 21.4 us -> 0 us
  local copies, waits for them, and re-layouts: 23.9 us -> 2.97 us
  between operations: 13.5 us -> 0.01 us
    pallas_call x0 -> x1, Pallas kernels: none -> 173 us  [body(): pl.pallas_call(functools.partial(kernel, cap), out_shape=jax.ShapeDtypeSt...]
    all_to_all x2 -> x0, waiting for transfers between devices: 134 us -> none  [the longest x1 134 us: body(): lax.all_to_all(send_rows.reshape(shards, capacity, width), 'vocab', split...]
    reduce_scatter x1 -> x0, waiting for transfers between devices: 98.2 us -> none  [body(): return lax.psum_scatter(partial_sum, 'dp', scatter_dimension=1, tiled=True)]
    scatter-add x1 -> x0, other arithmetic: 33.1 us -> none  [body(): jax.ops.segment_sum(got_rows.astype(jnp.float32), got_ids, num_segments=VSH)]
    scatter x2 -> x0, local copies, waits for them, and re-layouts: 22.3 us -> none  [the longest x1 14.2 us: body(): jnp.zeros((shards * capacity, width), jnp.bfloat16).at[slot]]
    all_to_all x2 -> x0, starting transfers between devices: 21.2 us -> none  [the longest x1 11.9 us: body(): lax.all_to_all(send_ids.reshape(shards, capacity), 'vocab', split_axis=0,...]
    another operation x3 -> x0, other arithmetic: 9.41 us -> none
  transfers between devices with their start and end apart: 3 -> 0, of which waited for: 2 -> 0; matrix products, arithmetic and copies ran while one was open for 5% -> 0% of each run, Pallas kernels for 0% -> 0%
where the time goes in v1:
time: 176 us
  Pallas kernels  173 us (98%)
  local copies, waits for them, and re-layouts  2.97 us (2%)
    pallas_call x1, Pallas kernels, body(): pl.pallas_call(functools.partial(kernel, cap), out_shape=jax.ShapeDtypeSt...  173 us

profile of v1, /device:TPU:1, one launch (start us, length us, event | category | flops | bytes accessed | tf_op | source)
XLA Modules:
  0.0 176.2 jit_solution(14038448940135842057)
XLA Ops:
  0.0 173.2 %delta_grad.1 = f32[3912,128]{1,0:T(8,128)} custom-call(s32[1,2048]{1,0:T(1,128)} %bitcast.1, bf16[2048,1024]{1,0:T(8,128)(2,1)} %grads_ref.1), custom_call_target="tpu_custom_call" | custom-call | tf_op jit(solution)/shard_map/delta_grad/pallas_call | solution.py:197
  173.2 3.0 %copy.4 = f32[3912,128]{1,0:T(8,128)} copy(f32[3912,128]{1,0:T(8,128)} %delta_grad.1) | data formatting | bytes 4005888

commit v2 on v1

v2 whole, which is shorter than its diff:
```python
import functools

import jax
import jax.numpy as jnp
from jax import lax
from jax.experimental import pallas as pl
from jax.experimental.pallas import tpu as pltpu
from jax.sharding import PartitionSpec as P

MESH = pl.DeviceIdType.MESH
VSH = 3912
SHARDS = 32
ROWS = 2048
DIRECT = 64
REST = 32
EXTRA = 32
CHUNK = 784
CHUNKS = 5
QUARTER = 256
HALF = 128
BATCHES = 8
PEERS = 128
NEAR = 32
PARTS = 2
THROTTLE = 8


def place():
    dp, vocab = lax.axis_index("dp"), lax.axis_index("vocab")
    return dp // 2, dp % 2, vocab // 4, vocab % 4


def offset(b, i):
    return 2 * i + b % 2, b // 2


def target(b, i, dy):
    y, c, z, x = place()
    dz, dx = offset(b, i)
    to_z, to_x, to_y = (z + dz) % 8, (x + dx) % 4, (y + dy) % 4
    return (to_y * 2 + c, to_z * 4 + to_x), to_y, to_z * 4 + to_x


def running(marks, before, carry):
    count = jnp.dot(marks.astype(jnp.bfloat16), before, preferred_element_type=jnp.float32) + carry
    return count, carry + jnp.sum(marks, axis=1, keepdims=True)


def rank_rows(ids_ref, rank, extra, parts):
    ids = ids_ref[...]
    first = lax.broadcasted_iota(jnp.int32, (SHARDS, 1), 0) * VSH
    local = ids - first
    marks = jnp.where((local >= 0) & (local < VSH), 1.0, 0.0)
    row = lax.broadcasted_iota(jnp.int32, (16, ROWS), 0)
    split = jnp.where(row == 0, ids >> 12, jnp.where(row == 1, (ids >> 6) & 63, jnp.where(row == 2, ids & 63, 0)))
    parts[...] = split.astype(jnp.float32).astype(jnp.bfloat16)
    block = 256
    before = lax.broadcasted_iota(jnp.int32, (block, block), 0) < lax.broadcasted_iota(jnp.int32, (block, block), 1)
    before = jnp.where(before, 1.0, 0.0).astype(jnp.bfloat16)
    carry = jnp.zeros((SHARDS, 1), jnp.float32)
    total = jnp.zeros((16, 1), jnp.float32)
    for k in range(ROWS // block):
        m = marks[:, k * block : (k + 1) * block]
        count, carry = running(m, before, carry)
        count = jnp.where(m > 0.5, count, -1.0)
        rank[:, k * block : (k + 1) * block] = count.astype(jnp.int32)
        over = jnp.sum(jnp.where(count >= DIRECT, 1.0, 0.0), axis=0, keepdims=True)
        over = jnp.broadcast_to(over, (16, block))
        place_of, total = running(over, before, total)
        place_of = jnp.where(over > 0.5, place_of, -1.0).astype(jnp.int32)
        extra[:, k * block : (k + 1) * block] = place_of[0:8]
    return total[0:1]


def kernel(main, cap, *refs):
    if main:
        (ids_ref, grads_hbm, out_ref, flag_ref), refs = refs[:4], refs[4:]
    else:
        (ids_ref, grads_hbm, sum_ref, out_ref), refs = refs[:4], refs[4:]
    grads_ref, lsem, rank, extra, parts, send, send_ids, recv, recv_ids, acc, other, ssem, isem, rsem, jsem, psem, qsem = refs[:17]
    if main:
        far_send, far, fs, fr, gs, gr = refs[17:]
    y, c, z, x = place()
    partner = (y * 2 + 1 - c, z * 4 + x)
    shard = z * 4 + x
    barrier = pltpu.get_barrier_semaphore()

    load = pltpu.make_async_copy(grads_hbm, grads_ref, lsem)
    load.start()
    planes = [(z + dz) % 8 * 4 for dz in range(8)]
    lines = [(x + dx) % 4 for dx in range(4)]
    groups = [(y + dy) % 4 * 2 + c for dy in range(4)]
    for j in range(1, PEERS):
        dz, dx, dy = j // 16, j // 4 % 4, j % 4
        peer = (groups[dy], planes[dz] + lines[dx])
        pl.semaphore_signal(barrier, inc=1, device_id=peer, device_id_type=MESH)
    pl.semaphore_signal(barrier, inc=1, device_id=partner, device_id_type=MESH)
    total = rank_rows(ids_ref, rank, extra, parts)
    send_ids[...] = jnp.zeros_like(send_ids)
    if main:
        spare = jnp.where(extra[0:1, :] >= 0, extra[0:1, :], EXTRA)
        pick_far = jnp.where(spare == lax.broadcasted_iota(jnp.int32, (EXTRA, ROWS), 0), 1.0, 0.0).astype(jnp.bfloat16)
    else:
        late = extra[0:1, :] >= EXTRA
        rank[...] = jnp.where(late & (rank[...] >= DIRECT), rank[...] - DIRECT, -1)
    def rows_copy(b, i, dy):
        peer, _, _ = target(b, i, dy)
        j = b * 16 + i * 4 + dy
        return pltpu.make_async_remote_copy(send.at[j], recv.at[j], ssem.at[j], rsem.at[j], device_id=peer, device_id_type=MESH)

    def ids_copy(b, i, dy):
        peer, _, _ = target(b, i, dy)
        j = b * 16 + i * 4 + dy
        return pltpu.make_async_remote_copy(
            send_ids.at[b * 4 + i], recv_ids.at[j], isem.at[j], jsem.at[j], device_id=peer, device_id_type=MESH
        )

    def far_copy(j):
        peer, _, _ = target(j // 16, j // 4 % 4, j % 4)
        return pltpu.make_async_remote_copy(far_send.at[j % 4], far.at[0, j], fs.at[j], fr.at[j], device_id=peer, device_id_type=MESH)

    def onward(part, dx):
        n = NEAR // PARTS
        s = part * 3 + dx - 1
        return pltpu.make_async_remote_copy(
            far.at[0, pl.ds(part * n, n)],
            far.at[dx, pl.ds(part * n, n)],
            gs.at[s],
            gr.at[s],
            device_id=(y * 2 + c, z * 4 + (x + dx) % 4),
            device_id_type=MESH,
        )

    own_rows = pltpu.make_async_copy(send.at[0], recv.at[0], rsem.at[0])
    own_ids = pltpu.make_async_copy(send_ids.at[0], recv_ids.at[0], jsem.at[0])

    def ids_of(pick):
        three = lax.dot_general(parts[...], pick, (((1,), (1,)), ((), ())), preferred_element_type=jnp.float32)
        return (three[0:1] * 4096.0 + three[1:2] * 64.0 + three[2:3]).astype(jnp.int32)

    if main:
        far_ids = ids_of(pick_far)
        for k in range(SHARDS):
            send_ids[k, :, cap : cap + EXTRA] = far_ids
            send_ids[k, :, 127:128] = jnp.where(total > EXTRA, 1, 0)
        load.wait()
        for dy in range(4):
            _, to_y, _ = target(0, 0, dy)
            cols = pl.ds(pl.multiple_of(to_y * QUARTER, QUARTER), QUARTER)
            packed = jnp.dot(pick_far, grads_ref[:, cols], preferred_element_type=jnp.float32).astype(jnp.bfloat16)
            far_send[dy] = packed
        pl.semaphore_wait(barrier, PEERS)
        own_far = pltpu.make_async_copy(far_send.at[0], far.at[0, 0], fr.at[0])
        own_far.start()

        def send_far(j, _):
            far_copy(j).start()
            return 0

        lax.fori_loop(1, NEAR, send_far, 0)
    else:
        load.wait()
        pl.semaphore_wait(barrier, PEERS)

    def pack(b, _):
        if THROTTLE < BATCHES:

            @pl.when(b >= THROTTLE)
            def _():
                lax.fori_loop(jnp.where(b == THROTTLE, 1, 0), 16, lambda k, _: sent((b - THROTTLE) * 16 + k, 0), 0)

        picks = []
        slot = lax.broadcasted_iota(jnp.int32, (cap, ROWS), 0)
        for i in range(4):
            _, _, to_shard = target(b, i, 0)
            pick = jnp.where(rank[pl.ds(to_shard, 1), :] == slot, 1.0, 0.0).astype(jnp.bfloat16)
            send_ids[b * 4 + i, :, 0:cap] = ids_of(pick) - to_shard * VSH
            picks.append(pick)
        picks = jnp.concatenate(picks, axis=0)
        for dy in range(4):
            _, to_y, _ = target(b, 0, dy)
            cols = pl.ds(pl.multiple_of(to_y * QUARTER, QUARTER), QUARTER)
            packed = jnp.dot(picks, grads_ref[:, cols], preferred_element_type=jnp.float32).astype(jnp.bfloat16)
            for i in range(4):
                send[b * 16 + i * 4 + dy] = packed[i * cap : (i + 1) * cap]
                if i == 0 and dy == 0:

                    @pl.when(b == 0)
                    def _():
                        own_rows.start()
                        own_ids.start()

                    @pl.when(b > 0)
                    def _():
                        ids_copy(b, 0, 0).start()
                        rows_copy(b, 0, 0).start()
                else:
                    ids_copy(b, i, dy).start()
                    rows_copy(b, i, dy).start()
        return 0

    def sent(j, _):
        rows_copy(j // 16, j // 4 % 4, j % 4).wait_send()
        ids_copy(j // 16, j // 4 % 4, j % 4).wait_send()
        return 0

    def add(block, t, ids, fresh=False):
        start = pl.multiple_of(t * CHUNK, 16)
        row = lax.broadcasted_iota(jnp.int32, (CHUNK, block.shape[0]), 0)
        hit = jnp.where(row == ids - start, 1.0, 0.0).astype(jnp.bfloat16)
        part = jnp.dot(hit, block, preferred_element_type=jnp.float32)
        rows = pl.ds(start, CHUNK)
        if fresh:
            acc[0, rows] = part[:, :HALF]
            acc[1, rows] = part[:, HALF:]
        else:
            acc[0, rows] += part[:, :HALF]
            acc[1, rows] += part[:, HALF:]

    def rows_of(b):
        return recv[pl.ds(b * 16, 16)].reshape(16 * cap, QUARTER)

    def arrive(b, ids=True, rows=True):
        def wait(k, _):
            if rows:
                rows_copy(b, k // 4, k % 4).wait_recv()
            if ids:
                ids_copy(b, k // 4, k % 4).wait_recv()
            return 0

        if isinstance(b, int) and b == 0:
            own_rows.wait()
            own_ids.wait()
            lax.fori_loop(1, 16, wait, 0)
        else:
            lax.fori_loop(0, 16, wait, 0)

    def ids_of_batch(b):
        return jnp.concatenate([recv_ids[b * 16 + k][:, 0:cap] for k in range(16)], axis=1)

    def exchange(t):
        rows = pl.ds(pl.multiple_of(t * CHUNK, 16), CHUNK)
        return pltpu.make_async_remote_copy(
            acc.at[1 - c, rows], other.at[rows], psem.at[t], qsem.at[t], device_id=partner, device_id_type=MESH
        )

    def sweep(block, ids, fresh=False, then=None):
        def step(t, ids):
            add(block(), t, ids, fresh)
            if then is not None:
                then(t)
            return ids

        lax.fori_loop(0, CHUNKS, step, ids)

    def batch(b, _):
        arrive(b)
        sweep(lambda: rows_of(b), ids_of_batch(b))
        return 0

    def far_block(dx):
        ids = [recv_ids[dx * NEAR + k][:, cap : cap + EXTRA] for k in range(NEAR)]
        ids = jnp.concatenate(ids, axis=1) - shard * VSH
        sweep(lambda: far[dx].reshape(NEAR * EXTRA, QUARTER), ids)

    lax.fori_loop(0, BATCHES, pack, 0)
    arrive(0)
    sweep(lambda: rows_of(0), ids_of_batch(0), fresh=True)
    if main:
        for part in range(PARTS):
            if part == 0:
                own_far.wait()
            lax.fori_loop(max(1, part * NEAR // PARTS), (part + 1) * NEAR // PARTS, lambda j, _: far_copy(j).wait_recv() or 0, 0)
            for dx in (1, 2, 3):
                onward(part, dx).start()
        batch(1, 0)
        far_block(0)
        for dx in (1, 2, 3):
            lax.fori_loop(2 * dx, 2 * dx + 2 if dx < 3 else 7, batch, 0)
            for part in range(PARTS):
                onward(part, dx).wait_recv()
            if dx == 3:
                arrive(7, rows=False)
            far_block(dx)
        worst = functools.reduce(jnp.maximum, [recv_ids[j][:, 127:128] for j in range(PEERS)])
        mark = jnp.broadcast_to(worst.astype(jnp.float32), (8, HALF))

        def then(t):
            @pl.when(t == CHUNKS - 1)
            def _():
                acc[1 - c, VSH : VSH + 8] = mark

            exchange(t).start()

        arrive(7, ids=False)
        sweep(lambda: rows_of(7), ids_of_batch(7), then=then)
    else:
        lax.fori_loop(1, 7, batch, 0)
        arrive(7)
        sweep(lambda: rows_of(7), ids_of_batch(7), then=lambda t: exchange(t).start())

    for t in range(CHUNKS):
        exchange(t).wait()
        a, n = t * CHUNK, min(CHUNK, VSH - t * CHUNK)
        result = acc[c, a : a + n] + other[a : a + n]
        out_ref[a : a + n] = result if main else sum_ref[a : a + n] + result
    if main:
        flag_ref[...] = jnp.maximum(mark, other[VSH : VSH + 8]).astype(jnp.int32)
        for part in range(PARTS):
            for dx in (1, 2, 3):
                onward(part, dx).wait_send()
        lax.fori_loop(1, NEAR, lambda j, _: far_copy(j).wait_send() or 0, 0)
    lax.fori_loop(max(1, (BATCHES - THROTTLE) * 16), PEERS, sent, 0)


def call(main, cap, *operands):
    shape = jax.ShapeDtypeStruct((VSH, HALF), jnp.float32)
    dma = pltpu.SemaphoreType.DMA
    scratch = [
        pltpu.VMEM((ROWS, 4 * QUARTER), jnp.bfloat16),
        dma,
        pltpu.VMEM((SHARDS, ROWS), jnp.int32),
        pltpu.VMEM((8, ROWS), jnp.int32),
        pltpu.VMEM((16, ROWS), jnp.bfloat16),
        pltpu.VMEM((PEERS, cap, QUARTER), jnp.bfloat16),
        pltpu.VMEM((SHARDS, 1, 128), jnp.int32),
        pltpu.VMEM((PEERS, cap, QUARTER), jnp.bfloat16),
        pltpu.VMEM((PEERS, 1, 128), jnp.int32),
        pltpu.VMEM((2, CHUNK * CHUNKS, HALF), jnp.float32),
        pltpu.VMEM((CHUNK * CHUNKS, HALF), jnp.float32),
    ] + [dma((PEERS,))] * 4 + [dma((CHUNKS,))] * 2
    if main:
        scratch += [
            pltpu.VMEM((4, EXTRA, QUARTER), jnp.bfloat16),
            pltpu.VMEM((4, NEAR, EXTRA, QUARTER), jnp.bfloat16),
        ] + [dma((NEAR,))] * 2 + [dma((3 * PARTS,))] * 2
    return pl.pallas_call(
        functools.partial(kernel, main, cap),
        out_shape=(shape, jax.ShapeDtypeStruct((8, HALF), jnp.int32)) if main else shape,
        in_specs=[pl.BlockSpec(memory_space=pl.ANY if k == 1 else pltpu.VMEM) for k in range(len(operands))],
        out_specs=[pl.BlockSpec(memory_space=pltpu.VMEM)] * 2 if main else pl.BlockSpec(memory_space=pltpu.VMEM),
        scratch_shapes=scratch,
        compiler_params=pltpu.CompilerParams(
            collective_id=0 if main else 1, has_side_effects=True, vmem_limit_bytes=56 << 20
        ),
        name="direct_rows" if main else "rest_rows",
    )(*operands)


def body(token_grads, token_ids):
    ids = token_ids.reshape(1, ROWS)
    sums, flag = call(True, DIRECT, ids, token_grads)
    return lax.cond(
        flag[0, 0] > 0,
        lambda ids, grads, sums: call(False, REST, ids, grads, sums),
        lambda ids, grads, sums: sums,
        ids,
        token_grads,
        sums,
    )


def solution(mesh):
    return jax.shard_map(
        body,
        mesh=mesh,
        in_specs=(P(("dp", "vocab"), None), P(("dp", "vocab"))),
        out_specs=P("vocab", "dp"),
        check_vma=False,
    )
```

time: 176 us -> 140 us (0.80)
  Pallas kernels: 173 us -> 136 us
    pallas_call x1, Pallas kernels: 173 us -> 136 us  [call(): pl.pallas_call(functools.partial(kernel, main, cap), out_shape=(shape, ja...]
where the time goes in v2:
time: 140 us
  Pallas kernels  136 us (97%)
  local copies, waits for them, and re-layouts  2.48 us (2%)
    pallas_call x1, Pallas kernels, call(): pl.pallas_call(functools.partial(kernel, main, cap), out_shape=(shape, ja...  136 us

profile of v2, /device:TPU:1, one launch (start us, length us, event | category | flops | bytes accessed | tf_op | source)
XLA Modules:
  0.0 139.7 jit_solution(3708777840206076770)
XLA Ops:
  0.0 0.0 copy-start
  0.0 0.0 copy-start.1
  0.0 136.4 %direct_rows.1 = (f32[3912,128]{1,0:T(8,128)S(1)}, s32[8,128]{1,0:T(8,128)}) custom-call(s32[1,2048]{1,0:T(1,128)} %bitcast.2, bf16[2048,1024]{1,0:T(8,128)(2,1)} %refs_1_.1), custom_call_target="tpu_custom_call" | custom-call | tf_op jit(solution)/shard_map/direct_rows/pallas_call | solution.py:337
  136.4 1.2 slice.3
  138.2 0.0 copy-done
  138.2 0.0 copy-done.1
  138.3 0.2 conditional.1
  138.5 1.3 copy.10
Async XLA Ops:
  0.0 138.2 %copy-start = (bf16[2048,1024]{1,0:T(8,128)(2,1)S(1)}, bf16[2048,1024]{1,0:T(8,128)(2,1)}, u32[]{:S(2)}) copy-start(bf16[2048,1024]{1,0:T(8,128)(2,1)} %refs_1_.1) | copy-start | bytes 12582916
  0.0 138.2 %copy-start.1 = (s32[2048]{0:T(1024)S(1)}, s32[2048]{0:T(1024)}, u32[]{:S(2)}) copy-start(s32[2048]{0:T(1024)} %param.5) | copy-start | bytes 24580

commit v3 on v2

--- a/solution.py
+++ b/solution.py
@@ -20,9 +20,9 @@
 HALF = 128
 BATCHES = 8
 PEERS = 128
-NEAR = 32
-PARTS = 2
-THROTTLE = 8
+BLOCKS = 32
+ORDER = (0, 3, 5, 1, 6, 4, 7, 2)
+HOPS = ((0, 1, 1), (5, 6, 1), (3, 4, 1), (0, 7, 7), (3, 2, 7), (5, 4, 7))
 
 
 def place():
@@ -74,12 +74,12 @@
 
 def kernel(main, cap, *refs):
     if main:
-        (ids_ref, grads_hbm, out_ref, flag_ref), refs = refs[:4], refs[4:]
+        (ids_ref, grads_hbm, out_hbm, flag_ref), refs = refs[:4], refs[4:]
     else:
-        (ids_ref, grads_hbm, sum_ref, out_ref), refs = refs[:4], refs[4:]
-    grads_ref, lsem, rank, extra, parts, send, send_ids, recv, recv_ids, acc, other, ssem, isem, rsem, jsem, psem, qsem = refs[:17]
-    if main:
-        far_send, far, fs, fr, gs, gr = refs[17:]
+        (ids_ref, grads_hbm, sum_ref, out_hbm), refs = refs[:4], refs[4:]
+    grads_ref, lsem, rank, extra, parts, send, send_ids, recv, recv_ids, acc, other, ssem, isem, rsem, jsem, psem, qsem, osem, own = refs[:19]
+    if main:
+        far_send, far, fs, fr, zs, zr, gs, gr = refs[19:]
     y, c, z, x = place()
     partner = (y * 2 + 1 - c, z * 4 + x)
     shard = z * 4 + x
@@ -103,43 +103,70 @@
     else:
         late = extra[0:1, :] >= EXTRA
         rank[...] = jnp.where(late & (rank[...] >= DIRECT), rank[...] - DIRECT, -1)
+    def slot_of(b, i):
+        return b + jnp.where(b == BATCHES - 1, i // 2, 0)
+
+    def settle(ref, start, count, sem):
+        span = ref.at[pl.ds(start, count)]
+        pltpu.make_async_copy(span, span, sem).wait()
+
     def rows_copy(b, i, dy):
         peer, _, _ = target(b, i, dy)
         j = b * 16 + i * 4 + dy
-        return pltpu.make_async_remote_copy(send.at[j], recv.at[j], ssem.at[j], rsem.at[j], device_id=peer, device_id_type=MESH)
+        return pltpu.make_async_remote_copy(send.at[j], recv.at[j], ssem.at[b], rsem.at[slot_of(b, i)], device_id=peer, device_id_type=MESH)
 
     def ids_copy(b, i, dy):
         peer, _, _ = target(b, i, dy)
         j = b * 16 + i * 4 + dy
         return pltpu.make_async_remote_copy(
-            send_ids.at[b * 4 + i], recv_ids.at[j], isem.at[j], jsem.at[j], device_id=peer, device_id_type=MESH
+            send_ids.at[b * 4 + i], recv_ids.at[j], isem.at[b], jsem.at[b], device_id=peer, device_id_type=MESH
         )
 
-    def far_copy(j):
-        peer, _, _ = target(j // 16, j // 4 % 4, j % 4)
-        return pltpu.make_async_remote_copy(far_send.at[j % 4], far.at[0, j], fs.at[j], fr.at[j], device_id=peer, device_id_type=MESH)
+    def far_copy(p, dy):
+        source = far_send.at[dy - 1] if dy else far.at[0, 0]
+        peer = ((y + dy) % 4 * 2 + c, (z + ORDER[p]) % 8 * 4 + x)
+        return pltpu.make_async_remote_copy(source, far.at[0, p * 4 + dy], fs, fr, device_id=peer, device_id_type=MESH)
+
+    def far_hop(k):
+        took, gives, dz = HOPS[k]
+        first, count = (0, 4) if gives != 4 else (0, 2) if dz == 1 else (2, 2)
+        return pltpu.make_async_remote_copy(
+            far.at[0, pl.ds(ORDER.index(took) * 4 + first, count)],
+            far.at[0, pl.ds(ORDER.index(gives) * 4 + first, count)],
+            zs.at[k],
+            zr.at[k],
+            device_id=(y * 2 + c, (z + dz) % 8 * 4 + x),
+            device_id_type=MESH,
+        )
 
     def onward(part, dx):
-        n = NEAR // PARTS
+        span = pl.ds(0, 12) if part == 0 else pl.ds(12, 20)
         s = part * 3 + dx - 1
         return pltpu.make_async_remote_copy(
-            far.at[0, pl.ds(part * n, n)],
-            far.at[dx, pl.ds(part * n, n)],
+            far.at[0, span],
+            far.at[dx, span],
             gs.at[s],
             gr.at[s],
             device_id=(y * 2 + c, z * 4 + (x + dx) % 4),
             device_id_type=MESH,
         )
 
-    own_rows = pltpu.make_async_copy(send.at[0], recv.at[0], rsem.at[0])
-    own_ids = pltpu.make_async_copy(send_ids.at[0], recv_ids.at[0], jsem.at[0])
-
-    def ids_of(pick):
+    def forward():
+        settle(far.at[0], 1, 11, fr)
+        for k in range(len(HOPS)):
+            far_hop(k).start()
+        for dx in (1, 2, 3):
+            onward(0, dx).start()
+
+    own_rows = pltpu.make_async_copy(send.at[0], recv.at[0], own.at[0])
+    own_ids = pltpu.make_async_copy(send_ids.at[0], recv_ids.at[0], own.at[1])
+
+    def ids_by(pick):
         three = lax.dot_general(parts[...], pick, (((1,), (1,)), ((), ())), preferred_element_type=jnp.float32)
         return (three[0:1] * 4096.0 + three[1:2] * 64.0 + three[2:3]).astype(jnp.int32)
 
     if main:
-        far_ids = ids_of(pick_far)
+        far_ids = ids_by(pick_far)
         for k in range(SHARDS):
             send_ids[k, :, cap : cap + EXTRA] = far_ids
             send_ids[k, :, 127:128] = jnp.where(total > EXTRA, 1, 0)
@@ -148,33 +175,28 @@
             _, to_y, _ = target(0, 0, dy)
             cols = pl.ds(pl.multiple_of(to_y * QUARTER, QUARTER), QUARTER)
             packed = jnp.dot(pick_far, grads_ref[:, cols], preferred_element_type=jnp.float32).astype(jnp.bfloat16)
-            far_send[dy] = packed
+            if dy == 0:
+                far[0, 0] = packed
+            else:
+                far_send[dy - 1] = packed
         pl.semaphore_wait(barrier, PEERS)
-        own_far = pltpu.make_async_copy(far_send.at[0], far.at[0, 0], fr.at[0])
-        own_far.start()
-
-        def send_far(j, _):
-            far_copy(j).start()
-            return 0
-
-        lax.fori_loop(1, NEAR, send_far, 0)
+        for p in range(3):
+            for dy in range(4):
+                if p + dy:
+                    far_copy(p, dy).start()
     else:
         load.wait()
         pl.semaphore_wait(barrier, PEERS)
 
     def pack(b, _):
-        if THROTTLE < BATCHES:
-
-            @pl.when(b >= THROTTLE)
-            def _():
-                lax.fori_loop(jnp.where(b == THROTTLE, 1, 0), 16, lambda k, _: sent((b - THROTTLE) * 16 + k, 0), 0)
-
+        if main:
+            pl.when(b == 2)(forward)
         picks = []
         slot = lax.broadcasted_iota(jnp.int32, (cap, ROWS), 0)
         for i in range(4):
             _, _, to_shard = target(b, i, 0)
             pick = jnp.where(rank[pl.ds(to_shard, 1), :] == slot, 1.0, 0.0).astype(jnp.bfloat16)
-            send_ids[b * 4 + i, :, 0:cap] = ids_of(pick) - to_shard * VSH
+            send_ids[b * 4 + i, :, 0:cap] = ids_by(pick) - to_shard * VSH
             picks.append(pick)
         picks = jnp.concatenate(picks, axis=0)
         for dy in range(4):
@@ -199,10 +221,17 @@
                     rows_copy(b, i, dy).start()
         return 0
 
-    def sent(j, _):
-        rows_copy(j // 16, j // 4 % 4, j % 4).wait_send()
-        ids_copy(j // 16, j // 4 % 4, j % 4).wait_send()
-        return 0
+    def sent():
+        for b in range(BATCHES):
+            settle(send, b * 16 + (b == 0), 16 - (b == 0), ssem.at[b])
+            settle(recv_ids, b * 16 + (b == 0), 16 - (b == 0), isem.at[b])
+        if main:
+            settle(far.at[0], 1, 11, fs)
+            for k in range(len(HOPS)):
+                far_hop(k).wait_send()
+            for part in range(2):
+                for dx in (1, 2, 3):
+                    onward(part, dx).wait_send()
 
     def add(block, t, ids, fresh=False):
         start = pl.multiple_of(t * CHUNK, 16)
@@ -217,26 +246,15 @@
             acc[0, rows] += part[:, :HALF]
             acc[1, rows] += part[:, HALF:]
 
-    def rows_of(b):
-        return recv[pl.ds(b * 16, 16)].reshape(16 * cap, QUARTER)
-
-    def arrive(b, ids=True, rows=True):
-        def wait(k, _):
-            if rows:
-                rows_copy(b, k // 4, k % 4).wait_recv()
-            if ids:
-                ids_copy(b, k // 4, k % 4).wait_recv()
-            return 0
-
-        if isinstance(b, int) and b == 0:
-            own_rows.wait()
-            own_ids.wait()
-            lax.fori_loop(1, 16, wait, 0)
-        else:
-            lax.fori_loop(0, 16, wait, 0)
-
-    def ids_of_batch(b):
-        return jnp.concatenate([recv_ids[b * 16 + k][:, 0:cap] for k in range(16)], axis=1)
+    def rows_of(b, start=0, stop=16):
+        return recv[pl.ds(b * 16 + start, stop - start)].reshape((stop - start) * cap, QUARTER)
+
+    def arrive(b):
+        settle(recv, b * 16, 16, rsem.at[b])
+        settle(recv_ids, b * 16, 16, jsem.at[b])
+
+    def ids_of(b, start=0, stop=16):
+        return jnp.concatenate([recv_ids[b * 16 + k][:, 0:cap] for k in range(start, stop)], axis=1)
 
     def exchange(t):
         rows = pl.ds(pl.multiple_of(t * CHUNK, 16), CHUNK)
@@ -255,32 +273,34 @@
 
     def batch(b, _):
         arrive(b)
-        sweep(lambda: rows_of(b), ids_of_batch(b))
+        sweep(lambda: rows_of(b), ids_of(b))
         return 0
 
     def far_block(dx):
-        ids = [recv_ids[dx * NEAR + k][:, cap : cap + EXTRA] for k in range(NEAR)]
+        at = [dx * 32 + r % 2 * 16 + r // 2 * 4 + dy for r in ORDER for dy in range(4)]
+        ids = [recv_ids[j][:, cap : cap + EXTRA] for j in at]
         ids = jnp.concatenate(ids, axis=1) - shard * VSH
-        sweep(lambda: far[dx].reshape(NEAR * EXTRA, QUARTER), ids)
+        sweep(lambda: far[dx].reshape(BLOCKS * EXTRA, QUARTER), ids)
 
     lax.fori_loop(0, BATCHES, pack, 0)
-    arrive(0)
-    sweep(lambda: rows_of(0), ids_of_batch(0), fresh=True)
-    if main:
-        for part in range(PARTS):
-            if part == 0:
-                own_far.wait()
-            lax.fori_loop(max(1, part * NEAR // PARTS), (part + 1) * NEAR // PARTS, lambda j, _: far_copy(j).wait_recv() or 0, 0)
-            for dx in (1, 2, 3):
-                onward(part, dx).start()
+    own_rows.wait()
+    own_ids.wait()
+    settle(recv, 1, 15, rsem.at[0])
+    settle(recv_ids, 1, 15, jsem.at[0])
+    sweep(lambda: rows_of(0), ids_of(0), fresh=True)
+    if main:
+        for k in range(len(HOPS)):
+            far_hop(k).wait_recv()
+        for dx in (1, 2, 3):
+            onward(1, dx).start()
         batch(1, 0)
         far_block(0)
         for dx in (1, 2, 3):
             lax.fori_loop(2 * dx, 2 * dx + 2 if dx < 3 else 7, batch, 0)
-            for part in range(PARTS):
+            for part in range(2):
                 onward(part, dx).wait_recv()
             if dx == 3:
-                arrive(7, rows=False)
+                settle(recv_ids, 112, 16, jsem.at[7])
             far_block(dx)
         worst = functools.reduce(jnp.maximum, [recv_ids[j][:, 127:128] for j in range(PEERS)])
         mark = jnp.broadcast_to(worst.astype(jnp.float32), (8, HALF))
@@ -292,25 +312,31 @@
 
             exchange(t).start()
 
-        arrive(7, ids=False)
-        sweep(lambda: rows_of(7), ids_of_batch(7), then=then)
+        settle(recv, 112, 8, rsem.at[7])
+        sweep(lambda: rows_of(7, stop=8), ids_of(7, stop=8))
+        sent()
+        settle(recv, 120, 8, rsem.at[8])
+        sweep(lambda: rows_of(7, start=8), ids_of(7, start=8), then=then)
     else:
         lax.fori_loop(1, 7, batch, 0)
-        arrive(7)
-        sweep(lambda: rows_of(7), ids_of_batch(7), then=lambda t: exchange(t).start())
-
+        settle(recv_ids, 112, 16, jsem.at[7])
+        settle(recv, 112, 8, rsem.at[7])
+        settle(recv, 120, 8, rsem.at[8])
+        sent()
+        sweep(lambda: rows_of(7), ids_of(7), then=lambda t: exchange(t).start())
+
+    stores = []
     for t in range(CHUNKS):
         exchange(t).wait()
         a, n = t * CHUNK, min(CHUNK, VSH - t * CHUNK)
+        if main and t == CHUNKS - 1:
+            flag_ref[0] = jnp.max(jnp.maximum(mark, other[VSH : VSH + 8])).astype(jnp.int32)
         result = acc[c, a : a + n] + other[a : a + n]
-        out_ref[a : a + n] = result if main else sum_ref[a : a + n] + result
-    if main:
-        flag_ref[...] = jnp.maximum(mark, other[VSH : VSH + 8]).astype(jnp.int32)
-        for part in range(PARTS):
-            for dx in (1, 2, 3):
-                onward(part, dx).wait_send()
-        lax.fori_loop(1, NEAR, lambda j, _: far_copy(j).wait_send() or 0, 0)
-    lax.fori_loop(max(1, (BATCHES - THROTTLE) * 16), PEERS, sent, 0)
+        other[a : a + n] = result if main else sum_ref[a : a + n] + result
+        stores.append(pltpu.make_async_copy(other.at[pl.ds(a, n)], out_hbm.at[pl.ds(a, n)], osem.at[t]))
+        stores[t].start()
+    for store in stores:
+        store.wait()
 
 
 def call(main, cap, *operands):
@@ -328,17 +354,18 @@
         pltpu.VMEM((PEERS, 1, 128), jnp.int32),
         pltpu.VMEM((2, CHUNK * CHUNKS, HALF), jnp.float32),
         pltpu.VMEM((CHUNK * CHUNKS, HALF), jnp.float32),
-    ] + [dma((PEERS,))] * 4 + [dma((CHUNKS,))] * 2
+    ] + [dma((BATCHES + 1,))] * 4 + [dma((CHUNKS,))] * 3 + [dma((2,))]
     if main:
         scratch += [
-            pltpu.VMEM((4, EXTRA, QUARTER), jnp.bfloat16),
-            pltpu.VMEM((4, NEAR, EXTRA, QUARTER), jnp.bfloat16),
-        ] + [dma((NEAR,))] * 2 + [dma((3 * PARTS,))] * 2
+            pltpu.VMEM((3, EXTRA, QUARTER), jnp.bfloat16),
+            pltpu.VMEM((4, BLOCKS, EXTRA, QUARTER), jnp.bfloat16),
+        ] + [dma] * 2 + [dma((6,))] * 4
+    whole = pl.BlockSpec(memory_space=pl.ANY)
     return pl.pallas_call(
         functools.partial(kernel, main, cap),
-        out_shape=(shape, jax.ShapeDtypeStruct((8, HALF), jnp.int32)) if main else shape,
-        in_specs=[pl.BlockSpec(memory_space=pl.ANY if k == 1 else pltpu.VMEM) for k in range(len(operands))],
-        out_specs=[pl.BlockSpec(memory_space=pltpu.VMEM)] * 2 if main else pl.BlockSpec(memory_space=pltpu.VMEM),
+        out_shape=(shape, jax.ShapeDtypeStruct((1,), jnp.int32)) if main else shape,
+        in_specs=[whole if k == 1 else pl.BlockSpec(memory_space=pltpu.VMEM) for k in range(len(operands))],
+        out_specs=[whole, pl.BlockSpec(memory_space=pltpu.SMEM)] if main else whole,
         scratch_shapes=scratch,
         compiler_params=pltpu.CompilerParams(
             collective_id=0 if main else 1, has_side_effects=True, vmem_limit_bytes=56 << 20
@@ -351,7 +378,7 @@
     ids = token_ids.reshape(1, ROWS)
     sums, flag = call(True, DIRECT, ids, token_grads)
     return lax.cond(
-        flag[0, 0] > 0,
+        flag[0] > 0,
         lambda ids, grads, sums: call(False, REST, ids, grads, sums),
         lambda ids, grads, sums: sums,
         ids,

time: 140 us -> 129 us (0.921)
  Pallas kernels: 136 us -> 127 us
    pallas_call x1, Pallas kernels: 136 us -> 127 us  [call(): pl.pallas_call(functools.partial(kernel, main, cap), out_shape=(shape, ja...]
where the time goes in v3:
time: 129 us
  Pallas kernels  127 us (98%)
  local copies, waits for them, and re-layouts  1.29 us (1%)
    pallas_call x1, Pallas kernels, call(): pl.pallas_call(functools.partial(kernel, main, cap), out_shape=(shape, ja...  127 us

profile of v3, /device:TPU:1, one launch (start us, length us, event | category | flops | bytes accessed | tf_op | source)
XLA Modules:
  0.0 128.7 jit_solution(380190924121818421)
XLA Ops:
  0.0 0.0 copy-start
  0.0 0.0 copy-start.1
  0.0 126.6 %direct_rows.1 = (f32[3912,128]{1,0:T(8,128)S(1)}, s32[1]{0:T(128)}) custom-call(s32[1,2048]{1,0:T(1,128)} %bitcast.2, bf16[2048,1024]{1,0:T(8,128)(2,1)} %refs_1_.1), custom_call_target="tpu_custom_call" | custom-call | tf_op jit(solution)/shard_map/direct_rows/pallas_call | solution.py:364
  127.2 0.0 copy-done
  127.2 0.0 copy-done.1
  127.2 0.2 conditional.1
  127.4 1.3 copy.10
Async XLA Ops:
  0.0 127.2 %copy-start = (bf16[2048,1024]{1,0:T(8,128)(2,1)S(1)}, bf16[2048,1024]{1,0:T(8,128)(2,1)}, u32[]{:S(2)}) copy-start(bf16[2048,1024]{1,0:T(8,128)(2,1)} %refs_1_.1) | copy-start | bytes 12582916
  0.0 127.2 %copy-start.1 = (s32[2048]{0:T(1024)S(1)}, s32[2048]{0:T(1024)}, u32[]{:S(2)}) copy-start(s32[2048]{0:T(1024)} %param.5) | copy-start | bytes 24580

commit v4 on v3

--- a/solution.py
+++ b/solution.py
@@ -190,7 +190,7 @@
 
     def pack(b, _):
         if main:
-            pl.when(b == 2)(forward)
+            pl.when(b == 1)(forward)
         picks = []
         slot = lax.broadcasted_iota(jnp.int32, (cap, ROWS), 0)
         for i in range(4):
@@ -314,7 +314,6 @@
 
         settle(recv, 112, 8, rsem.at[7])
         sweep(lambda: rows_of(7, stop=8), ids_of(7, stop=8))
-        sent()
         settle(recv, 120, 8, rsem.at[8])
         sweep(lambda: rows_of(7, start=8), ids_of(7, start=8), then=then)
     else:
@@ -335,6 +334,8 @@
         other[a : a + n] = result if main else sum_ref[a : a + n] + result
         stores.append(pltpu.make_async_copy(other.at[pl.ds(a, n)], out_hbm.at[pl.ds(a, n)], osem.at[t]))
         stores[t].start()
+    if main:
+        sent()
     for store in stores:
         store.wait()
 

time: 129 us -> 129 us (level)
  no operation moved by 1% of the time
where the time goes in v4:
time: 129 us; the launch traced here: 128 us
  Pallas kernels  126 us (98%)
  local copies, waits for them, and re-layouts  1.29 us (1%)
    pallas_call x1, Pallas kernels, call(): pl.pallas_call(functools.partial(kernel, main, cap), out_shape=(shape, ja...  126 us

profile of v4, /device:TPU:1, one launch (start us, length us, event | category | flops | bytes accessed | tf_op | source)
XLA Modules:
  0.0 128.5 jit_solution(9851978463742457960)
XLA Ops:
  0.0 0.0 copy-start
  0.0 0.0 copy-start.1
  0.0 126.3 %direct_rows.1 = (f32[3912,128]{1,0:T(8,128)S(1)}, s32[1]{0:T(128)}) custom-call(s32[1,2048]{1,0:T(1,128)} %bitcast.2, bf16[2048,1024]{1,0:T(8,128)(2,1)} %refs_1_.1), custom_call_target="tpu_custom_call" | custom-call | tf_op jit(solution)/shard_map/direct_rows/pallas_call | solution.py:365
  127.0 0.0 copy-done
  127.0 0.0 copy-done.1
  127.0 0.2 conditional.1
  127.2 1.3 %copy.10 = f32[3912,128]{1,0:T(8,128)} copy(f32[3912,128]{1,0:T(8,128)S(1)} %get-tuple-element.22) | data formatting | bytes 4005888
Async XLA Ops:
  0.0 127.0 %copy-start = (bf16[2048,1024]{1,0:T(8,128)(2,1)S(1)}, bf16[2048,1024]{1,0:T(8,128)(2,1)}, u32[]{:S(2)}) copy-start(bf16[2048,1024]{1,0:T(8,128)(2,1)} %refs_1_.1) | copy-start | bytes 12582916
  0.0 127.0 %copy-start.1 = (s32[2048]{0:T(1024)S(1)}, s32[2048]{0:T(1024)}, u32[]{:S(2)}) copy-start(s32[2048]{0:T(1024)} %param.5) | copy-start | bytes 24580
